TPU v7x, 512 devices: a whole 4x8x8 slice. The times are simulated.
512 devices in a mesh: wide: 32 (over y_lo, z), tp: 16 (over y_hi, x, core).
Axes of the slice: x: 4, y: 8 (y_hi: 2, y_lo: 4; y = y_hi * 4 + y_lo), z: 8, core: 2. Of those that a mesh axis runs over, the one named last changes fastest.
Arguments:
- hidden_in: bfloat16 [64, 16384], P(None, 'wide'), may hold values from -6 to 6
- q_weight: bfloat16 [16384, 16384], P('wide', 'tp'), may hold values from -0.046875 to 0.046875
- kv_weight: bfloat16 [16384, 2048], P('wide', 'tp'), may hold values from -0.046875 to 0.046875
- o_weight: bfloat16 [16384, 16384], P('tp', 'wide'), may hold values from -0.046875 to 0.046875
- cache_keys: bfloat16 [64, 1024, 1024], P('tp', 'wide'), may hold values from -1000 to 1000, as said below
- cache_values: bfloat16 [64, 1024, 1024], P('tp', 'wide'), may hold values from -6 to 6
- lengths: int32 [64], P('tp'), may hold values from 1 to 1024, as said below
- positions: int32 [64], P('tp'), may hold values from 0 to 8191
Outputs:
- attended: bfloat16 [64, 16384], P('tp', 'wide')
- new_kv: bfloat16 [64, 2048], P('tp')
Inputs may be any that keep to these rules, and one draw needn't show every extreme that they name: `cache_keys`: keys already carry the rotary embedding of their positions. Row b's cache holds valid entries in its first lengths[b] rows; some row fills all 1024.
All inputs are finite; a program needn't handle non-finite values.
Results may differ from a plain program's by a relative error of at most 0.015.
The roundings to bfloat16 on the way count: a program that leaves them out, or rounds other values in their place, can miss the bound.
Values may be sent and summed in bfloat16 or wider, within the bound.
No kernel may reach another device: no remote copies, remote signals or barrier semaphores. Data moves between devices by JAX's collectives and lax.ppermute only.
A program may use at most 64 MiB of HBM per device.

v0:
```python
import jax
import jax.numpy as jnp
from jax import lax
from jax.sharding import PartitionSpec as P

NH = 128
KVH = 8
DH = 128


LOWEST = -1e30


def joined_2(array, axis, combine):
    everything = jax.tree.map(lambda part: lax.all_gather(part, axis), array)
    initial = jax.tree.map(lambda part: part[0], everything)

    def turn(k, so_far):
        return combine(so_far, jax.tree.map(lambda part: part[k], everything))

    return lax.fori_loop(1, lax.axis_size(axis), turn, initial)


def rotate(block, positions):
    half = block.shape[-1] // 2
    freq = 500000.0 ** (-(jnp.arange(half, dtype=jnp.float32) * 2.0 / block.shape[-1]))
    angle = positions.astype(jnp.float32)[:, None] * freq[None, :]
    cosine = jnp.cos(angle)[:, None, :]
    sine = jnp.sin(angle)[:, None, :]
    first = block[..., :half]
    second = block[..., half:]
    return jnp.concatenate([first * cosine - second * sine, second * cosine + first * sine], -1)


def combine_states(earlier, later):
    top_a, total_a, mixed_a = earlier
    top_b, total_b, mixed_b = later
    highest = jnp.maximum(top_a, top_b)
    scale_a = jnp.exp(top_a - highest)
    scale_b = jnp.exp(top_b - highest)
    total = total_a * scale_a + total_b * scale_b
    mixed = mixed_a * scale_a[..., None] + mixed_b * scale_b[..., None]
    return (highest, total, mixed)


def per_device(
    hidden_in, q_weight, kv_weight, o_weight, cache_keys, cache_values, lengths, positions
):
    width_q = q_weight.shape[1]
    seq_here = lengths.shape[0]
    tp_count = lax.axis_size("tp")
    groups = NH // KVH
    factor = DH ** (-0.5)
    partial_sum = jnp.concatenate(
        [
            jnp.dot(hidden_in, q_weight, preferred_element_type=jnp.float32),
            jnp.dot(hidden_in, kv_weight, preferred_element_type=jnp.float32),
        ],
        1,
    )
    joined = lax.psum(partial_sum, "wide").astype(jnp.bfloat16)
    arrived = lax.all_to_all(joined, "tp", split_axis=0, concat_axis=1, tiled=True).reshape(
        seq_here, tp_count, -1
    )
    query_raw = arrived[:, :, :width_q].reshape(seq_here, NH, DH)
    fresh = arrived[:, :, width_q:].reshape(seq_here, 2 * KVH * DH)
    query = (
        rotate(query_raw.astype(jnp.float32), positions)
        .astype(jnp.bfloat16)
        .reshape(seq_here, KVH, groups, DH)
    )
    new_keys = rotate(
        fresh[:, : KVH * DH].astype(jnp.float32).reshape(seq_here, KVH, DH), positions
    ).astype(jnp.bfloat16)
    new_values = fresh[:, KVH * DH :].reshape(seq_here, KVH, DH)
    new_kv = jnp.concatenate([new_keys.reshape(seq_here, KVH * DH), fresh[:, KVH * DH :]], 1)
    span = cache_keys.shape[1]
    keys = cache_keys.reshape(seq_here, span, KVH, DH)
    values = cache_values.reshape(seq_here, span, KVH, DH)
    scores = jnp.einsum("skgd,sckd->skgc", query, keys, preferred_element_type=jnp.float32) * factor
    own = jnp.einsum("skgd,skd->skg", query, new_keys, preferred_element_type=jnp.float32) * factor
    wide_index = lax.axis_index("wide")
    places = wide_index * span + jnp.arange(span, dtype=jnp.int32)
    valid = (places[None, :] < lengths[:, None])[:, None, None, :]
    leader = wide_index == 0
    top = jnp.maximum(jnp.max(jnp.where(valid, scores, LOWEST), -1), jnp.where(leader, own, LOWEST))
    weight = jnp.where(valid, jnp.exp(scores - top[..., None]), 0.0)
    weight_own = jnp.where(leader, jnp.exp(own - top), 0.0)
    total = jnp.sum(weight, -1) + weight_own
    mixed = jnp.einsum(
        "skgc,sckd->skgd", weight.astype(jnp.bfloat16), values, preferred_element_type=jnp.float32
    )
    mixed = (
        mixed
        + weight_own.astype(jnp.bfloat16).astype(jnp.float32)[..., None]
        * new_values.astype(jnp.float32)[:, :, None, :]
    )
    top = top.reshape(seq_here, NH)
    total = total.reshape(seq_here, NH)
    mixed = mixed.reshape(seq_here, NH, DH)
    top_all, total_all, mixed_all = joined_2((top, total, mixed), "wide", combine_states)
    attention = (mixed_all / total_all[..., None]).astype(jnp.bfloat16)
    flat = attention.reshape(seq_here, NH * DH)
    spread = lax.all_to_all(flat, "tp", split_axis=1, concat_axis=0, tiled=True)
    attended = lax.psum_scatter(
        jnp.dot(spread, o_weight, preferred_element_type=jnp.float32),
        "tp",
        scatter_dimension=0,
        tiled=True,
    ).astype(jnp.bfloat16)
    return (attended, new_kv)


def solution(mesh):
    in_specs = (
        P(None, "wide"),
        P("wide", "tp"),
        P("wide", "tp"),
        P("tp", "wide"),
        P("tp", "wide", None),
        P("tp", "wide", None),
        P("tp"),
        P("tp"),
    )
    out_specs = (P("tp", "wide"), P("tp", None))
    return jax.shard_map(
        per_device, mesh=mesh, in_specs=in_specs, out_specs=out_specs, check_vma=False
    )
```

profile of v0, /device:TPU:1, one launch (start us, length us, event | category | flops | bytes accessed | tf_op | source)
XLA Modules:
  0.0 499.8 jit_solution(5746440457092670419)
XLA Ops:
  7.2 1.2 fusion.24
  8.5 1.1 fusion.23
  9.7 135.6 %all-reduce.3 = bf16[64,1152]{1,0:T(8,128)(2,1)S(1)} all-reduce(f32[64,1152]{1,0:T(8,128)S(1)} %pad_maximum_fusion), channel_id=1, replica_groups=mesh['wide'=32,'tp'=16] {'wide'}, use_global_device_ids=true, to_apply=%region_0.0 | all-reduce | flops 73728 | bytes 442368 | tf_op jit(solution)/shard_map/psum | solution.py:61
  145.2 0.7 all_to_all.26
  145.9 35.1 %all-to-all-start = ((bf16[16,4,1152]{2,1,0:T(4,128)(2,1)}), bf16[16,4,1152]{2,1,0:T(4,128)(2,1)S(1)}, u32[]{:S(2)}, u32[]{:S(2)}) async-start(bf16[16,4,1152]{2,1,0:T(4,128)(2,1)} %all_to_all.26), calls=%async_computation | async-start | bytes 294912 | tf_op jit(solution)/shard_map/all_to_all | solution.py:62
  181.1 0.7 broadcast_compare_fusion
  181.9 0.7 convert_element_type.51
  182.5 0.1 multiply_cosine_fusion
  182.7 8.7 %all-to-all-done = bf16[16,4,1152]{2,1,0:T(4,128)(2,1)S(1)} async-done(((bf16[16,4,1152]{2,1,0:T(4,128)(2,1)}), bf16[16,4,1152]{2,1,0:T(4,128)(2,1)S(1)}, u32[]{:S(2)}, u32[]{:S(2)}) %all-to-all-start) | async-done | bytes 147488 | tf_op jit(solution)/shard_map/all_to_all | solution.py:62
  191.5 0.1 multiply_subtract_fusion
  191.6 0.1 subtract_convert_fusion
  191.7 0.1 fusion.22
  191.8 0.2 fusion.13
  192.0 1.3 select_reduce_fusion
  193.4 0.3 fusion.8
  193.7 2.0 convolution_add_fusion
  195.7 1.3 dynamic-slice
  197.6 0.1 all_gather_reshape.9
  197.7 0.1 all_gather_reshape.10
  197.8 62.4 %all_gather.10 = f32[32,4,128]{2,1,0:T(4,128)S(1)} all-gather(f32[1,4,128]{2,1,0:T(4,128)S(1)} %all_gather_reshape.10), channel_id=1, replica_groups=mesh['wide'=32,'tp'=16] {'wide'}, dimensions={0}, use_global_device_ids=true | all-gather | bytes 67584 | tf_op jit(solution)/shard_map/all_gather | solution.py:15
  260.2 63.3 %all_gather.9 = f32[32,4,128]{2,1,0:T(4,128)S(1)} all-gather(f32[1,4,128]{2,1,0:T(4,128)S(1)} %all_gather_reshape.9), channel_id=1, replica_groups=mesh['wide'=32,'tp'=16] {'wide'}, dimensions={0}, use_global_device_ids=true | all-gather | bytes 67584 | tf_op jit(solution)/shard_map/all_gather | solution.py:15
  323.5 12.8 %all-gather.2.cloned.1.call-done = f32[32,4,128,128]{3,2,1,0:T(8,128)} async-done(((f32[1,4,128,128]{3,2,1,0:T(8,128)}), f32[32,4,128,128]{3,2,1,0:T(8,128)}) %all-gather.2.cloned.1.call-update) | async-done | bytes 8388624 | tf_op jit(solution)/shard_map/all_gather | solution.py:15
  336.3 1.0 slice_bitcast_fusion
  337.2 39.0 %while.19 = (s32[]{:T(128)}, f32[4,128]{1,0:T(4,128)S(1)}, f32[4,128]{1,0:T(4,128)S(1)}, f32[4,128,128]{2,1,0:T(8,128)S(1)}, f32[32,4,128]{2,1,0:T(4,128)S(1)}, ...) while((s32[]{:T(128)}, f32[4,128]{1,0:T(4,128)S(1)}, ...), condition=%wide.region_4.5_spmd, body=%wide.region_3.4_spmd.sunk | while | flops 199685 | bytes 807055 | solution.py:21
  337.3 1.2 fusion.37
  338.6 1.2 fusion.37
  339.8 1.2 fusion.37
  341.1 1.2 fusion.37
  342.3 1.2 fusion.37
  343.6 1.2 fusion.37
  344.8 1.2 fusion.37
  346.1 1.2 fusion.37
  347.4 1.2 fusion.37
  348.6 1.2 fusion.37
  349.9 1.2 fusion.37
  351.1 1.2 fusion.37
  352.4 1.2 fusion.37
  353.7 1.2 fusion.37
  354.9 1.2 fusion.37
  356.2 1.2 fusion.37
  357.4 1.2 fusion.37
  358.7 1.2 fusion.37
  359.9 1.2 fusion.37
  361.2 1.2 fusion.37
  362.5 1.2 fusion.37
  363.7 1.2 fusion.37
  365.0 1.2 fusion.37
  366.2 1.2 fusion.37
  367.5 1.2 fusion.37
  368.8 1.2 fusion.37
  370.0 1.2 fusion.37
  371.3 1.2 fusion.37
  372.5 1.2 fusion.37
  373.8 1.2 fusion.37
  375.0 1.2 fusion.37
  376.3 0.1 divide_convert_fusion
  376.5 0.8 copy.24
  377.2 26.7 %all-to-all-start.1 = ((bf16[4,16,1024]{2,0,1:T(4,128)(2,1)}), bf16[4,16,1024]{2,0,1:T(4,128)(2,1)S(1)}, u32[]{:S(2)}, u32[]{:S(2)}) async-start(bf16[4,16,1024]{2,0,1:T(4,128)(2,1)} %copy.24), calls=%async_computation.1 | async-start | bytes 262144 | tf_op jit(solution)/shard_map/all_to_all | solution.py:104
  404.0 0.1 fusion.21
  404.1 0.6 pad_maximum_fusion.4
  404.7 9.3 %all-to-all-done.1 = bf16[4,16,1024]{2,0,1:T(4,128)(2,1)S(1)} async-done(((bf16[4,16,1024]{2,0,1:T(4,128)(2,1)}), bf16[4,16,1024]{2,0,1:T(4,128)(2,1)S(1)}, u32[]{:S(2)}, u32[]{:S(2)}) %all-to-all-start.1) | async-done | bytes 131104 | tf_op jit(solution)/shard_map/all_to_all | solution.py:104
  414.0 0.3 fusion.25
  414.3 78.0 %all-reduce.4 = bf16[64,512]{1,0:T(8,128)(2,1)S(1)} all-reduce(f32[64,512]{1,0:T(8,128)S(1)} %fusion.25), channel_id=2, replica_groups=mesh['wide'=32,'tp'=16] {'tp'}, use_global_device_ids=true, to_apply=%region_5.6.clone | all-reduce | flops 32768 | bytes 196608
  492.4 0.6 dynamic-slice_convert_fusion
  (54 shorter events, 1.3 us)
Async XLA Ops:
  7.2 1.3 copy-start
  7.2 406.8 %copy-start.1 = (bf16[1024,512]{1,0:T(8,128)(2,1)S(1)}, bf16[1024,512]{1,0:T(8,128)(2,1)}, u32[]{:S(2)}) copy-start(bf16[1024,512]{1,0:T(8,128)(2,1)} %param.13) | copy-start | bytes 3145732
  145.9 45.4 %all-to-all-start = ((bf16[16,4,1152]{2,1,0:T(4,128)(2,1)}), bf16[16,4,1152]{2,1,0:T(4,128)(2,1)S(1)}, u32[]{:S(2)}, u32[]{:S(2)}) async-start(bf16[16,4,1152]{2,1,0:T(4,128)(2,1)} %all_to_all.26), calls=%async_computation | async-start | bytes 294912 | tf_op jit(solution)/shard_map/all_to_all | solution.py:62
  181.1 155.2 %all-gather.2.cloned.1.call-start = ((), (), s32[]{:S(2)}) async-start(), calls=%async_computation.2 | async-start | bytes 8650752 | tf_op jit(solution)/shard_map/all_gather | solution.py:15
  377.2 36.8 %all-to-all-start.1 = ((bf16[4,16,1024]{2,0,1:T(4,128)(2,1)}), bf16[4,16,1024]{2,0,1:T(4,128)(2,1)S(1)}, u32[]{:S(2)}, u32[]{:S(2)}) async-start(bf16[4,16,1024]{2,0,1:T(4,128)(2,1)} %copy.24), calls=%async_computation.1 | async-start | bytes 262144 | tf_op jit(solution)/shard_map/all_to_all | solution.py:104
Sparse Core Ops, SparseCore 0:
  195.8 140.4 all-gather.1
where the time goes:
time: 508 us; the launch traced here: 500 us
  blocking collectives  339 us (67%)
  starting transfers between devices  61.9 us (12%)
  other arithmetic  41.2 us (8%)
  waiting for transfers between devices  30.7 us (6%)
  between operations  14.9 us (3%)
  matrix products  6.22 us (1%)
    psum x1, blocking collectives, per_device(): joined = lax.psum(partial_sum, 'wide').astype(jnp.bfloat16)  136 us
    all_gather x2, blocking collectives, joined_2(): everything = jax.tree.map(lambda part: lax.all_gather(part, axis), array)  126 us
    unnamed x1, blocking collectives  78 us
    add x31, other arithmetic, combine_states(): mixed = mixed_a * scale_a[..., None] + mixed_b * scale_b[..., None]  37.4 us
    all_to_all x1, starting transfers between devices, per_device(): lax.all_to_all(joined, 'tp', split_axis=0, concat_axis=1, tiled=True)  35.1 us
    all_to_all x1, starting transfers between devices, per_device(): spread = lax.all_to_all(flat, 'tp', split_axis=1, concat_axis=0, tiled=True)  26.7 us
    all_gather x1, waiting for transfers between devices, joined_2(): everything = jax.tree.map(lambda part: lax.all_gather(part, axis), array)  12.8 us
  transfers between devices with their start and end apart: 3, of which 3 were waited for; matrix products, arithmetic and copies ran while one was open for 1% of the time, Pallas kernels for 0%

commit v1 on v0

v1 whole, which is shorter than its diff:
```python
import jax
import jax.numpy as jnp
from jax import lax
from jax.sharding import Mesh
from jax.sharding import PartitionSpec as P

NH = 128
KVH = 8
DH = 128
GROUP = NH // KVH

LOWEST = -1e30

AXES = ("yl", "z", "yh", "x", "core")
SIZES = (4, 8, 2, 4, 2)
WIDE = ("yl", "z")
TP = ("yh", "x", "core")
ROWS = ("yl", "yh", "x", "core")


def exchange(array, axes):
    return lax.all_to_all(array, axes, split_axis=0, concat_axis=0, tiled=True)


def rotate(block, position):
    half = block.shape[-1] // 2
    freq = 500000.0 ** (-(jnp.arange(half, dtype=jnp.float32) * 2.0 / block.shape[-1]))
    angle = position.astype(jnp.float32) * freq
    cosine = jnp.cos(angle)
    sine = jnp.sin(angle)
    first = block[..., :half]
    second = block[..., half:]
    return jnp.concatenate([first * cosine - second * sine, second * cosine + first * sine], -1)


def per_device(
    hidden_in, q_weight, kv_weight, o_weight, cache_keys, cache_values, lengths, positions
):
    f32, bf16 = jnp.float32, jnp.bfloat16
    seqs, span = cache_keys.shape[:2]
    tp = 16

    partial = jnp.concatenate(
        [
            jnp.dot(hidden_in, q_weight, preferred_element_type=f32).astype(bf16),
            jnp.dot(hidden_in, kv_weight, preferred_element_type=f32).astype(bf16),
        ],
        1,
    ).reshape(tp, seqs, -1)
    partial = exchange(partial, TP)

    q_part = partial[:, :, : GROUP * DH // 2].reshape(KVH, 2, seqs, GROUP // 2, DH)
    q_part = q_part.transpose(2, 0, 1, 3, 4).reshape(seqs, KVH, GROUP, DH)
    kv_part = partial[:, :, GROUP * DH // 2 :].reshape(2, KVH, seqs, DH).transpose(2, 1, 0, 3)
    keys = cache_keys.reshape(seqs, span, KVH, DH).transpose(0, 2, 1, 3)
    values = cache_values.reshape(seqs, span, KVH, DH).transpose(0, 2, 1, 3)
    blank = jnp.zeros((seqs, KVH, 6, DH), bf16)
    packed = jnp.concatenate([keys, values, q_part, kv_part, blank], 2)
    packed = exchange(packed.reshape(seqs * KVH, -1, DH), WIDE)

    keys = packed[:, :span].reshape(-1, DH)
    values = packed[:, span : 2 * span].reshape(-1, DH)
    sums = jnp.sum(packed[:, 2 * span :].astype(f32), 0).astype(bf16)
    mine = lax.axis_index("yl")
    length = lengths[mine]
    position = positions[mine]
    turned = rotate(sums[: GROUP + 1].astype(f32), position).astype(bf16)
    query = turned[:GROUP]
    new_key = turned[GROUP]
    new_value = sums[GROUP + 1]

    factor = DH ** (-0.5)
    scores = jnp.dot(query, keys.T, preferred_element_type=f32) * factor
    own = jnp.dot(query, new_key, preferred_element_type=f32) * factor
    valid = (jnp.arange(keys.shape[0], dtype=jnp.int32) < length)[None, :]
    top = jnp.maximum(jnp.max(jnp.where(valid, scores, LOWEST), -1), own)
    weight = jnp.where(valid, jnp.exp(scores - top[:, None]), 0.0)
    weight_own = jnp.exp(own - top)
    total = jnp.sum(weight, -1) + weight_own
    mixed = jnp.dot(weight.astype(bf16), values, preferred_element_type=f32)
    mixed = mixed + weight_own.astype(bf16).astype(f32)[:, None] * new_value.astype(f32)[None, :]
    attention = (mixed / total[:, None]).astype(bf16)

    row = jnp.concatenate([attention, new_key[None], new_value[None], jnp.zeros((6, DH), bf16)], 0)
    heads = exchange(jnp.broadcast_to(row[None], (KVH,) + row.shape), ("z",))
    piece = jnp.concatenate(
        [
            heads[:, :GROUP].reshape(tp, GROUP // 2, DH),
            heads[:, GROUP : GROUP + 2].transpose(1, 0, 2).reshape(tp, 1, DH),
        ],
        1,
    )
    piece = jnp.broadcast_to(piece[None], (seqs,) + piece.shape).reshape(seqs * tp, -1, DH)
    piece = exchange(piece, ROWS)
    flat = piece[:, : GROUP // 2].reshape(seqs * tp, -1)
    product = jnp.dot(flat, o_weight, preferred_element_type=f32).astype(bf16)
    out = jnp.concatenate([product, piece[:, GROUP // 2]], 1)
    out = out.reshape(seqs, tp, -1).transpose(1, 0, 2)
    out = exchange(out, TP)
    width = o_weight.shape[1]
    attended = jnp.sum(out[:, :, :width].astype(f32), 0).astype(bf16)
    new_kv = out[:, :, width:].transpose(1, 0, 2).reshape(seqs, -1)
    return (attended, new_kv)


def solution(mesh):
    fine = Mesh(mesh.devices.reshape(SIZES), AXES)
    in_specs = (
        P(None, WIDE),
        P(WIDE, TP),
        P(WIDE, TP),
        P(TP, WIDE),
        P(TP, WIDE, None),
        P(TP, WIDE, None),
        P(TP),
        P(TP),
    )
    out_specs = (P(TP, WIDE), P(TP, None))
    return jax.shard_map(
        per_device, mesh=fine, in_specs=in_specs, out_specs=out_specs, check_vma=False
    )
```

time: 508 us -> 108 us (0.21); the launches traced: 500 us -> 107 us
  blocking collectives: 339 us -> 45.7 us
  other arithmetic: 41.2 us -> 1.91 us
  starting transfers between devices: 61.9 us -> 23.2 us
  between operations: 14.9 us -> 1.62 us
  waiting for transfers between devices: 30.7 us -> 24.8 us
    psum x1 -> x0, blocking collectives: 136 us -> none  [per_device(): joined = lax.psum(partial_sum, 'wide').astype(jnp.bfloat16)]
    all_gather x2 -> x0, blocking collectives: 126 us -> none  [joined_2(): everything = jax.tree.map(lambda part: lax.all_gather(part, axis), array)]
    unnamed x1 -> x0, blocking collectives: 78 us -> none
    all_to_all x0 -> x3, blocking collectives: none -> 45.7 us  [exchange(): return lax.all_to_all(array, axes, split_axis=0, concat_axis=0, tiled=True)]
    all_to_all x2, starting transfers between devices: 61.9 us -> 23.2 us  [exchange(): return lax.all_to_all(array, axes, split_axis=0, concat_axis=0, tiled=True)]
    add x63 -> x1, other arithmetic: 38.3 us -> 0.01 us  [per_device(): total = jnp.sum(weight, -1) + weight_own]
    all_gather x1 -> x0, waiting for transfers between devices: 12.8 us -> none  [joined_2(): everything = jax.tree.map(lambda part: lax.all_gather(part, axis), array)]
    all_to_all x2, waiting for transfers between devices: 18 us -> 24.8 us  [exchange(): return lax.all_to_all(array, axes, split_axis=0, concat_axis=0, tiled=True)]
  transfers between devices with their start and end apart: 3 -> 2, of which waited for: 3 -> 2; matrix products, arithmetic and copies ran while one was open for 1% -> 2% of each run, Pallas kernels for 0% -> 0%
where the time goes in v1:
time: 108 us; the launch traced here: 107 us
  blocking collectives  45.7 us (42%)
  waiting for transfers between devices  24.8 us (23%)
  starting transfers between devices  23.2 us (21%)
  local copies, waits for them, and re-layouts  7.78 us (7%)
  matrix products  2.52 us (2%)
  other arithmetic  1.91 us (2%)
  between operations  1.62 us (2%)
    all_to_all x3, blocking collectives, exchange(): return lax.all_to_all(array, axes, split_axis=0, concat_axis=0, tiled=True)  45.7 us
    all_to_all x2, waiting for transfers between devices, exchange(): return lax.all_to_all(array, axes, split_axis=0, concat_axis=0, tiled=True)  24.8 us
    all_to_all x2, starting transfers between devices, exchange(): return lax.all_to_all(array, axes, split_axis=0, concat_axis=0, tiled=True)  23.2 us
    concatenate x3, local copies, waits for them, and re-layouts, per_device(): packed = jnp.concatenate([keys, values, q_part, kv_part, blank], 2)  2.96 us
  transfers between devices with their start and end apart: 2, of which 2 were waited for; matrix products, arithmetic and copies ran while one was open for 2% of the time, Pallas kernels for 0%

profile of v1, /device:TPU:1, one launch (start us, length us, event | category | flops | bytes accessed | tf_op | source)
XLA Modules:
  0.0 107.4 jit_solution(2887945453513958781)
XLA Ops:
  0.6 0.0 copy-start
  0.6 0.0 copy-start.2
  0.7 1.2 %convolution_convert_fusion.2 = bf16[64,128]{1,0:T(8,128)(2,1)S(1)} fusion(bf16[64,512]{1,0:T(8,128)(2,1)} %param.8, bf16[512,128]{1,0:T(8,128)(2,1)} %param.10), kind=kOutput, calls=%fused_computation.3 | convolution fusion | flops 8396800 | bytes 212992 | tf_op jit(solution)/shard_map/dot_general | solution.py:46
  1.8 0.1 copy-done
  2.0 0.0 copy-done.2
  2.0 0.3 convolution_convert_fusion
  2.3 0.0 copy-start.3
  2.3 0.7 reshape.75
  3.0 11.1 %all-to-all-start = ((bf16[16,4,1152]{2,1,0:T(4,128)(2,1)}), bf16[16,4,1152]{2,1,0:T(4,128)(2,1)S(1)}, u32[]{:S(2)}, u32[]{:S(2)}) async-start(bf16[16,4,1152]{2,1,0:T(4,128)(2,1)} %reshape.75), calls=%async_computation | async-start | bytes 294912 | tf_op jit(solution)/shard_map/all_to_all | solution.py:22
  14.1 0.0 copy-done.3
  14.2 0.0 copy-start.4
  14.2 0.9 copy-done.4
  15.2 9.1 %all-to-all-done = bf16[16,4,1152]{2,1,0:T(4,128)(2,1)S(1)} async-done(((bf16[16,4,1152]{2,1,0:T(4,128)(2,1)}), bf16[16,4,1152]{2,1,0:T(4,128)(2,1)S(1)}, u32[]{:S(2)}, u32[]{:S(2)}) %all-to-all-start) | async-done | bytes 147488 | tf_op jit(solution)/shard_map/all_to_all | solution.py:22
  24.4 0.1 reshape.88
  24.5 2.9 %concatenate.38 = bf16[32,88,128]{2,1,0:T(8,128)(2,1)} concatenate(bf16[32,32,128]{2,1,0:T(8,128)(2,1)S(1)} %bitcast.74, bf16[32,32,128]{2,1,0:T(8,128)(2,1)S(1)} %bitcast.75, bf16[32,16,128]{2,1,0:T(8,128)(2,1)S(1)} %bitcast.77, bf16[32,2,128]{2,1,0:T(2,128)(2,1)S(1)} %copy.27, bf16[32,6,128]{2,1,0:T(8,128)(2,1)S(1)} %broadcast_in_dim.46), dimensions={1} | concatenate | bytes 1441792 | tf_op jit(solution)/shard_map/concatenate | solution.py:58
  27.5 12.1 %all-to-all-start.1 = ((bf16[32,88,128]{2,1,0:T(8,128)(2,1)}), bf16[32,88,128]{2,1,0:T(8,128)(2,1)S(1)}, u32[]{:S(2)}, u32[]{:S(2)}) async-start(bf16[32,88,128]{2,1,0:T(8,128)(2,1)} %concatenate.38), calls=%async_computation.1 | async-start | bytes 1441792 | tf_op jit(solution)/shard_map/all_to_all | solution.py:22
  39.6 0.0 copy-start.5
  39.6 0.6 copy-done.5
  40.2 0.6 dynamic_slice.7
  40.8 0.0 copy-start.6
  41.5 0.0 copy-done.6
  41.5 0.6 dynamic_slice.6
  42.1 0.1 pad.7.clone
  42.2 0.7 iota_compare_fusion
  42.9 15.7 %all-to-all-done.1 = bf16[32,88,128]{2,1,0:T(8,128)(2,1)S(1)} async-done(((bf16[32,88,128]{2,1,0:T(8,128)(2,1)}), bf16[32,88,128]{2,1,0:T(8,128)(2,1)S(1)}, u32[]{:S(2)}, u32[]{:S(2)}) %all-to-all-start.1) | async-done | bytes 720928 | tf_op jit(solution)/shard_map/all_to_all | solution.py:22
  58.6 0.1 subtract_convert_fusion
  58.7 0.1 pad_maximum_fusion.2
  58.8 0.3 select_reduce_fusion
  59.2 0.2 convert_convert_fusion
  59.4 0.0 copy-start.1
  59.4 0.2 fusion.5
  59.6 0.2 fusion.1
  59.8 0.1 maximum_maximum_fusion
  59.9 11.9 %all_to_all.25 = bf16[8,24,128]{2,1,0:T(8,128)(2,1)S(1)} all-to-all(bf16[8,24,128]{2,1,0:T(8,128)(2,1)S(1)} %broadcast_in_dim.50), channel_id=1, replica_groups=mesh['yl'=4,'z'=8,'yh'=2,'x'=4,'core'=2] {'z'}, dimensions={0} | all-to-all | bytes 98304 | tf_op jit(solution)/shard_map/all_to_all | solution.py:22
  71.9 19.1 %all_to_all.26 = bf16[64,9,128]{2,1,0:T(8,128)(2,1)S(1)} all-to-all(bf16[64,9,128]{2,1,0:T(8,128)(2,1)S(1)} %bitcast.71), channel_id=1, replica_groups=mesh['yl'=4,'z'=8,'yh'=2,'x'=4,'core'=2] {'yl','yh','x','core'}, dimensions={0} | all-to-all | bytes 294912 | tf_op jit(solution)/shard_map/all_to_all | solution.py:22
  91.0 0.0 copy-done.1
  91.0 0.3 convolution_convert_fusion.1
  91.3 0.1 copy.31
  91.5 14.7 %all_to_all.27 = bf16[16,4,640]{2,1,0:T(4,128)(2,1)S(1)} all-to-all(bf16[16,4,640]{2,1,0:T(4,128)(2,1)S(1)} %maximum_bitcast_fusion), channel_id=1, replica_groups=mesh['yl'=4,'z'=8,'yh'=2,'x'=4,'core'=2] {'yh','x','core'}, dimensions={0} | all-to-all | bytes 163840 | tf_op jit(solution)/shard_map/all_to_all | solution.py:22
  106.2 0.6 slice_reduce_fusion.1
  106.8 0.6 slice_bitcast_fusion
  (32 shorter events, 0.7 us)
Async XLA Ops:
  0.6 1.3 %copy-start = (bf16[512,1024]{1,0:T(8,128)(2,1)S(1)}, bf16[512,1024]{1,0:T(8,128)(2,1)}, u32[]{:S(2)}) copy-start(bf16[512,1024]{1,0:T(8,128)(2,1)} %param.9) | copy-start | bytes 3145732
  0.6 1.3 %copy-start.2 = (bf16[64,512]{1,0:T(8,128)(2,1)S(1)}, bf16[64,512]{1,0:T(8,128)(2,1)}, u32[]{:S(2)}) copy-start(bf16[64,512]{1,0:T(8,128)(2,1)} %param.8) | copy-start | bytes 196612
  2.3 11.8 %copy-start.3 = (bf16[4,32,1024]{2,1,0:T(8,128)(2,1)S(1)}, bf16[4,32,1024]{2,1,0:T(8,128)(2,1)}, u32[]{:S(2)}) copy-start(bf16[4,32,1024]{2,1,0:T(8,128)(2,1)} %param.12) | copy-start | bytes 786436
  3.0 21.3 %all-to-all-start = ((bf16[16,4,1152]{2,1,0:T(4,128)(2,1)}), bf16[16,4,1152]{2,1,0:T(4,128)(2,1)S(1)}, u32[]{:S(2)}, u32[]{:S(2)}) async-start(bf16[16,4,1152]{2,1,0:T(4,128)(2,1)} %reshape.75), calls=%async_computation | async-start | bytes 294912 | tf_op jit(solution)/shard_map/all_to_all | solution.py:22
  14.2 1.0 copy-start.4
  27.5 31.1 %all-to-all-start.1 = ((bf16[32,88,128]{2,1,0:T(8,128)(2,1)}), bf16[32,88,128]{2,1,0:T(8,128)(2,1)S(1)}, u32[]{:S(2)}, u32[]{:S(2)}) async-start(bf16[32,88,128]{2,1,0:T(8,128)(2,1)} %concatenate.38), calls=%async_computation.1 | async-start | bytes 1441792 | tf_op jit(solution)/shard_map/all_to_all | solution.py:22
  39.6 0.7 copy-start.5
  40.8 0.7 copy-start.6
  59.4 31.7 %copy-start.1 = (bf16[1024,512]{1,0:T(8,128)(2,1)S(1)}, bf16[1024,512]{1,0:T(8,128)(2,1)}, u32[]{:S(2)}) copy-start(bf16[1024,512]{1,0:T(8,128)(2,1)} %param.11) | copy-start | bytes 3145732

commit v2 on v1

v2 whole, which is shorter than its diff:
```python
import functools

import jax
import jax.numpy as jnp
import numpy as np
from jax import lax
from jax.experimental import pallas as pl
from jax.experimental.pallas import tpu as pltpu
from jax.sharding import Mesh
from jax.sharding import PartitionSpec as P

NH = 128
KVH = 8
DH = 128
GROUP = NH // KVH
HALF = GROUP // 2

LOWEST = -1e30
LIMIT = 8 * 2**20

AXES = ("yl", "z", "yh", "x", "core")
SIZES = (4, 8, 2, 4, 2)
WIDE = ("yl", "z")
TP = ("yh", "x", "core")


def exchange(array, axes):
    return lax.all_to_all(array, axes, split_axis=0, concat_axis=0, tiled=True)


def frequencies():
    half = DH // 2
    power = -(np.arange(half, dtype=np.float32) * np.float32(2.0) / np.float32(DH))
    freq = np.power(np.float64(500000.0), power.astype(np.float64)).astype(np.float32)
    return np.concatenate([freq, freq])[None]


def call(kernel, out_shape, in_specs, name, **options):
    return pl.pallas_call(
        kernel,
        out_shape=out_shape,
        in_specs=in_specs,
        out_specs=jax.tree.map(lambda _: pl.BlockSpec(memory_space=pltpu.VMEM), out_shape),
        compiler_params=pltpu.CompilerParams(vmem_limit_bytes=LIMIT),
        name=name,
        **options,
    )


IN_VMEM = pl.BlockSpec(memory_space=pltpu.VMEM)


def prepare_kernel(
    keys_ref, values_ref, freq_ref, lengths_ref, positions_ref, packed_ref, turn_ref, valid_ref
):
    seqs, span = keys_ref.shape[:2]
    pairs = span // 2
    for seq in range(seqs):
        for head in range(KVH):
            place = seq * KVH + head
            columns = pl.ds(head * DH, DH)
            packed_ref[place, :pairs] = keys_ref[seq, :, columns].reshape(pairs, 2, DH)
            packed_ref[place, pairs : 2 * pairs] = values_ref[seq, :, columns].reshape(pairs, 2, DH)
    lane = lax.broadcasted_iota(jnp.int32, lengths_ref.shape, 1)
    chosen = lane == lax.axis_index("yl")
    length = jnp.sum(jnp.where(chosen, lengths_ref[...], 0), axis=1, keepdims=True)
    position = jnp.sum(jnp.where(chosen, positions_ref[...], 0), axis=1, keepdims=True)
    valid = lax.broadcasted_iota(jnp.int32, valid_ref.shape, 1) < length
    valid_ref[...] = valid.astype(jnp.float32)
    angle = position.astype(jnp.float32) * freq_ref[...]
    sine = jnp.sin(angle)
    first_half = lax.broadcasted_iota(jnp.int32, sine.shape, 1) < DH // 2
    turn_ref[0:1] = jnp.cos(angle)
    turn_ref[1:2] = jnp.where(first_half, -sine, sine)


def prepare(cache_keys, cache_values, freq, lengths, positions, rows, places):
    seqs = cache_keys.shape[0]
    return call(
        prepare_kernel,
        [
            jax.ShapeDtypeStruct((seqs * KVH, rows // 2, 2, DH), cache_keys.dtype),
            jax.ShapeDtypeStruct((2, DH), jnp.float32),
            jax.ShapeDtypeStruct((1, places), jnp.float32),
        ],
        [IN_VMEM] * 5,
        "prepare",
    )(cache_keys, cache_values, freq, lengths[None], positions[None])


def place_kernel(packed_ref, fresh_ref, out_ref):
    del packed_ref
    count, rows = fresh_ref.shape[:2]
    fresh = fresh_ref[...].reshape(count, rows // 2, 2, DH)
    out_ref[:, out_ref.shape[1] - rows // 2 :] = fresh


def place(packed, fresh):
    return call(
        place_kernel,
        jax.ShapeDtypeStruct(packed.shape, packed.dtype),
        [IN_VMEM] * 2,
        "place",
        input_output_aliases={0: 0},
    )(packed, fresh)


def attention_kernel(packed_ref, turn_ref, valid_ref, out_ref, *, span):
    f32, bf16 = jnp.float32, jnp.bfloat16
    sources = packed_ref.shape[0]
    pairs = span // 2
    sums = packed_ref[0, 2 * pairs :].reshape(-1, DH).astype(f32)
    for source in range(1, sources):
        sums = sums + packed_ref[source, 2 * pairs :].reshape(-1, DH).astype(f32)
    sums = sums.astype(bf16)
    plain = sums.astype(f32)
    swapped = pltpu.roll(plain, DH // 2, 1)
    turned = (plain * turn_ref[0:1] + swapped * turn_ref[1:2]).astype(bf16)
    query = turned[:GROUP]
    new_key = turned[GROUP : GROUP + 1]
    new_value = sums[GROUP + 1 : GROUP + 2]

    factor = DH ** (-0.5)
    keys = packed_ref[:, :pairs].reshape(-1, DH)
    values = packed_ref[:, pairs : 2 * pairs].reshape(-1, DH)
    scores = lax.dot_general(
        query, keys, (((1,), (1,)), ((), ())), preferred_element_type=f32
    ) * factor
    own = jnp.sum(query.astype(f32) * new_key.astype(f32), -1, keepdims=True) * factor
    valid = valid_ref[...] > 0
    top = jnp.maximum(jnp.max(jnp.where(valid, scores, LOWEST), -1, keepdims=True), own)
    weight = jnp.where(valid, jnp.exp(scores - top), 0.0)
    weight_own = jnp.exp(own - top)
    total = jnp.sum(weight, -1, keepdims=True) + weight_own
    mixed = jnp.dot(weight.astype(bf16), values, preferred_element_type=f32)
    mixed = mixed + weight_own.astype(bf16).astype(f32) * new_value.astype(f32)
    attention = (mixed / total).astype(bf16)

    for half, extra in enumerate((new_key, new_value)):
        first = half * HALF
        rows = jnp.concatenate([attention[first : first + HALF], extra, extra], 0)
        out_ref[:, half] = jnp.broadcast_to(rows[None], (out_ref.shape[0],) + rows.shape)


def attend(packed, turn, valid, span):
    return call(
        functools.partial(attention_kernel, span=span),
        jax.ShapeDtypeStruct((KVH, 2, HALF + 2, DH), jnp.bfloat16),
        [IN_VMEM] * 3,
        "attend",
    )(packed, turn, valid)


def finish_kernel(parts_ref, attended_ref, new_kv_ref):
    width = attended_ref.shape[1]
    sources = parts_ref.shape[0]
    sums = parts_ref[0, :, :width].astype(jnp.float32)
    for source in range(1, sources):
        sums = sums + parts_ref[source, :, :width].astype(jnp.float32)
    attended_ref[...] = sums.astype(attended_ref.dtype)
    for source in range(sources):
        column = (source % 2 * KVH + source // 2) * DH
        new_kv_ref[:, pl.ds(column, DH)] = parts_ref[source, :, width:]


def finish(parts, width):
    sources, seqs = parts.shape[:2]
    return call(
        finish_kernel,
        [
            jax.ShapeDtypeStruct((seqs, width), parts.dtype),
            jax.ShapeDtypeStruct((seqs, sources * DH), parts.dtype),
        ],
        [IN_VMEM],
        "finish",
    )(parts)


def per_device(
    hidden_in, q_weight, kv_weight, o_weight, cache_keys, cache_values, lengths, positions
):
    f32, bf16 = jnp.float32, jnp.bfloat16
    seqs, span = cache_keys.shape[:2]
    tp = lax.axis_size(TP)
    batch = hidden_in.shape[0]
    rows = 2 * span + GROUP + 2
    places = span * lax.axis_size(WIDE)

    packed, turn, valid = prepare(
        cache_keys, cache_values, frequencies(), lengths, positions, rows, places
    )
    q_part = jnp.dot(hidden_in, q_weight, preferred_element_type=f32).astype(bf16)
    kv_part = jnp.dot(hidden_in, kv_weight, preferred_element_type=f32).astype(bf16)
    partial = jnp.concatenate([q_part, kv_part], 1).reshape(tp, seqs, -1)
    partial, packed, turn, valid = lax.optimization_barrier((partial, packed, turn, valid))
    partial = exchange(partial, TP)

    q_rows = partial[:, :, : HALF * DH].reshape(KVH, 2, seqs, HALF, DH)
    q_rows = q_rows.transpose(2, 0, 1, 3, 4).reshape(seqs, KVH, GROUP, DH)
    kv_rows = partial[:, :, HALF * DH :].reshape(2, KVH, seqs, DH).transpose(2, 1, 0, 3)
    fresh = jnp.concatenate([q_rows, kv_rows], 2)
    packed = place(packed, fresh.reshape(seqs * KVH, -1, DH))
    packed = exchange(packed, WIDE)
    heads = attend(packed, turn, valid, span)

    heads = exchange(heads.reshape((KVH * 2,) + heads.shape[2:]), ("z", "core"))
    middle = HALF * DH // 2
    mixed = heads[:, :HALF].reshape(KVH, 2, 2, middle)
    fresh = heads[:, HALF : HALF + 2].reshape(KVH, 2, 2, DH)
    piece = jnp.concatenate([mixed, fresh], 3)
    piece = jnp.broadcast_to(piece[:, None], (KVH, seqs) + piece.shape[1:])
    piece = exchange(piece.reshape((KVH * seqs,) + piece.shape[2:]), ("yh", "x", "yl"))
    flat = jnp.concatenate([piece[:, :, 0, :middle], piece[:, :, 1, :middle]], 2)
    product = jnp.dot(flat.reshape(batch, -1), o_weight, preferred_element_type=f32).astype(bf16)
    out = jnp.concatenate([product, piece[:, :, 0, middle:].reshape(batch, -1)], 1)
    out = out.reshape(KVH, seqs, 2, -1).transpose(0, 2, 1, 3).reshape(tp, seqs, -1)
    out = exchange(out, TP)
    return finish(out, o_weight.shape[1])


def solution(mesh):
    fine = Mesh(mesh.devices.reshape(SIZES), AXES)
    in_specs = (
        P(None, WIDE),
        P(WIDE, TP),
        P(WIDE, TP),
        P(TP, WIDE),
        P(TP, WIDE, None),
        P(TP, WIDE, None),
        P(TP),
        P(TP),
    )
    out_specs = (P(TP, WIDE), P(TP, None))
    return jax.shard_map(
        per_device, mesh=fine, in_specs=in_specs, out_specs=out_specs, check_vma=False
    )
```

time: 108 us -> 100 us (0.926)
  blocking collectives: 45.7 us -> 93.8 us
  waiting for transfers between devices: 24.8 us -> 0 us
  starting transfers between devices: 23.2 us -> 0 us
  local copies, waits for them, and re-layouts: 7.78 us -> 1.66 us
  other arithmetic: 1.91 us -> 0.12 us
  Pallas kernels: 0 us -> 1.78 us
    all_to_all x3 -> x5, blocking collectives: 45.7 us -> 93.8 us  [exchange(): return lax.all_to_all(array, axes, split_axis=0, concat_axis=0, tiled=True)]
    all_to_all x2 -> x0, waiting for transfers between devices: 24.8 us -> none  [exchange(): return lax.all_to_all(array, axes, split_axis=0, concat_axis=0, tiled=True)]
    all_to_all x2 -> x0, starting transfers between devices: 23.2 us -> none  [exchange(): return lax.all_to_all(array, axes, split_axis=0, concat_axis=0, tiled=True)]
    concatenate x6 -> x5, local copies, waits for them, and re-layouts: 3.1 us -> 0.16 us  [the longest x2 0.07 us: per_device(): jnp.concatenate([piece[:, :, 0, :middle], piece[:, :, 1, :middle]], 2)]
    pallas_call x0 -> x4, Pallas kernels: none -> 1.78 us  [the longest x1 0.62 us: finish(): call(finish_kernel, [jax.ShapeDtypeStruct((seqs, width), parts.dtype), ja...]
    reshape x5 -> x4, local copies, waits for them, and re-layouts: 1.39 us -> 0.14 us  [the longest x2 0.08 us: per_device(): q_rows = partial[:, :, :HALF * DH].reshape(KVH, 2, seqs, HALF, DH)]
    dynamic_slice x2 -> x0, local copies, waits for them, and re-layouts: 1.17 us -> none  [the longest x1 0.59 us: per_device(): length = lengths[mine]]
  transfers between devices with their start and end apart: 2 -> 0, of which waited for: 2 -> 0; matrix products, arithmetic and copies ran while one was open for 2% -> 0% of each run, Pallas kernels for 0% -> 0%
where the time goes in v2:
time: 100 us
  blocking collectives  93.8 us (94%)
  Pallas kernels  1.78 us (2%)
  matrix products  1.77 us (2%)
  local copies, waits for them, and re-layouts  1.66 us (2%)
    all_to_all x5, blocking collectives, exchange(): return lax.all_to_all(array, axes, split_axis=0, concat_axis=0, tiled=True)  93.8 us

profile of v2, /device:TPU:1, one launch (start us, length us, event | category | flops | bytes accessed | tf_op | source)
XLA Modules:
  0.0 100.0 jit_solution(4806020580770824207)
XLA Ops:
  0.6 0.0 copy-start
  0.6 0.0 copy-start.7
  0.7 1.2 %convolution_convert_fusion.2 = bf16[64,128]{1,0:T(8,128)(2,1)S(1)} fusion(bf16[64,512]{1,0:T(8,128)(2,1)} %param.9, bf16[512,128]{1,0:T(8,128)(2,1)} %param.11), kind=kOutput, calls=%fused_computation.2 | convolution fusion | flops 8396800 | bytes 212992 | tf_op jit(solution)/shard_map/dot_general | solution.py:193
  1.8 0.1 copy-done
  2.0 0.0 copy-done.7
  2.0 0.3 convolution_convert_fusion
  2.3 0.0 copy-start.1
  2.3 0.0 copy-start.2
  2.4 0.0 copy-start.3
  2.4 0.0 copy-start.4
  2.4 0.0 copy-start.5
  2.4 0.8 copy-done.1
  3.2 0.1 copy-done.2
  3.3 0.0 copy-done.3
  3.3 0.0 copy-done.4
  3.3 0.0 copy-done.5
  3.3 0.5 prepare.1
  3.8 21.1 %all_to_all.25 = bf16[16,4,1152]{2,1,0:T(4,128)(2,1)S(1)} all-to-all(bf16[16,4,1152]{2,1,0:T(4,128)(2,1)S(1)} %reshape.43), channel_id=1, replica_groups=mesh['yl'=4,'z'=8,'yh'=2,'x'=4,'core'=2] {'yh','x','core'}, dimensions={0} | all-to-all | bytes 294912 | tf_op jit(solution)/shard_map/all_to_all | solution.py:28
  24.9 0.1 reshape.44
  25.1 0.1 place.1
  25.3 29.9 %all_to_all.26.packed_ref = bf16[32,41,2,128]{3,2,1,0:T(2,128)(2,1)S(1)} all-to-all(bf16[32,41,2,128]{3,2,1,0:T(2,128)(2,1)S(1)} %place.1), channel_id=1, replica_groups=mesh['yl'=4,'z'=8,'yh'=2,'x'=4,'core'=2] {'yl','z'}, dimensions={0} | all-to-all | bytes 1343488 | tf_op jit(solution)/shard_map/all_to_all | solution.py:28
  55.1 0.0 copy-start.6
  55.1 0.6 attend.1
  55.7 14.6 %all_to_all.27 = bf16[16,10,128]{2,1,0:T(8,128)(2,1)S(1)} all-to-all(bf16[16,10,128]{2,1,0:T(8,128)(2,1)S(1)} %bitcast.27), channel_id=1, replica_groups=mesh['yl'=4,'z'=8,'yh'=2,'x'=4,'core'=2] {'z','core'}, dimensions={0} | all-to-all | bytes 81920 | tf_op jit(solution)/shard_map/all_to_all | solution.py:28
  70.4 0.1 broadcast_in_dim.14
  70.5 14.0 %all_to_all.28 = bf16[32,2,2,640]{3,1,2,0:T(2,128)(2,1)S(1)} all-to-all(bf16[32,2,2,640]{3,1,2,0:T(2,128)(2,1)S(1)} %bitcast.30), channel_id=1, replica_groups=mesh['yl'=4,'z'=8,'yh'=2,'x'=4,'core'=2] {'yh','x','yl'}, dimensions={0} | all-to-all | bytes 327680 | tf_op jit(solution)/shard_map/all_to_all | solution.py:28
  84.5 0.1 fusion.4
  84.7 0.0 copy-done.6
  84.7 0.3 convolution_convert_fusion.1
  85.2 14.3 %all_to_all.29.parts_ref = bf16[16,4,640]{2,1,0:T(4,128)(2,1)S(1)} all-to-all(bf16[16,4,640]{2,1,0:T(4,128)(2,1)S(1)} %bitcast.32), channel_id=1, replica_groups=mesh['yl'=4,'z'=8,'yh'=2,'x'=4,'core'=2] {'yh','x','core'}, dimensions={0} | all-to-all | bytes 163840 | tf_op jit(solution)/shard_map/all_to_all | solution.py:28
  99.4 0.6 finish.1
  (20 shorter events, 0.5 us)
Async XLA Ops:
  0.6 1.3 %copy-start = (bf16[512,1024]{1,0:T(8,128)(2,1)S(1)}, bf16[512,1024]{1,0:T(8,128)(2,1)}, u32[]{:S(2)}) copy-start(bf16[512,1024]{1,0:T(8,128)(2,1)} %param.10) | copy-start | bytes 3145732
  0.6 1.3 %copy-start.7 = (bf16[64,512]{1,0:T(8,128)(2,1)S(1)}, bf16[64,512]{1,0:T(8,128)(2,1)}, u32[]{:S(2)}) copy-start(bf16[64,512]{1,0:T(8,128)(2,1)} %param.9) | copy-start | bytes 196612
  2.3 1.0 copy-start.1
  2.3 1.0 %copy-start.2 = (bf16[4,32,1024]{2,1,0:T(8,128)(2,1)S(1)}, bf16[4,32,1024]{2,1,0:T(8,128)(2,1)}, u32[]{:S(2)}) copy-start(bf16[4,32,1024]{2,1,0:T(8,128)(2,1)} %values_ref.1) | copy-start | bytes 786436
  2.4 0.9 copy-start.3
  2.4 0.9 copy-start.4
  2.4 0.9 copy-start.5
  55.1 29.6 %copy-start.6 = (bf16[1024,512]{1,0:T(8,128)(2,1)S(1)}, bf16[1024,512]{1,0:T(8,128)(2,1)}, u32[]{:S(2)}) copy-start(bf16[1024,512]{1,0:T(8,128)(2,1)} %param.12) | copy-start | bytes 3145732

commit v3 on v2

--- a/solution.py
+++ b/solution.py
@@ -192,7 +192,6 @@
     q_part = jnp.dot(hidden_in, q_weight, preferred_element_type=f32).astype(bf16)
     kv_part = jnp.dot(hidden_in, kv_weight, preferred_element_type=f32).astype(bf16)
     partial = jnp.concatenate([q_part, kv_part], 1).reshape(tp, seqs, -1)
-    partial, packed, turn, valid = lax.optimization_barrier((partial, packed, turn, valid))
     partial = exchange(partial, TP)
 
     q_rows = partial[:, :, : HALF * DH].reshape(KVH, 2, seqs, HALF, DH)

time: 100 us -> 99.8 us (level)
  blocking collectives: 93.8 us -> 72.7 us
  starting transfers between devices: 0 us -> 11.1 us
  waiting for transfers between devices: 0 us -> 9.08 us
    all_to_all x5 -> x4, blocking collectives: 93.8 us -> 72.7 us  [exchange(): return lax.all_to_all(array, axes, split_axis=0, concat_axis=0, tiled=True)]
    all_to_all x0 -> x1, starting transfers between devices: none -> 11.1 us  [exchange(): return lax.all_to_all(array, axes, split_axis=0, concat_axis=0, tiled=True)]
    all_to_all x0 -> x1, waiting for transfers between devices: none -> 9.08 us  [exchange(): return lax.all_to_all(array, axes, split_axis=0, concat_axis=0, tiled=True)]
  transfers between devices with their start and end apart: 0 -> 1, of which waited for: 0 -> 1; matrix products, arithmetic and copies ran while one was open for 0% -> 0% of each run, Pallas kernels for 0% -> 0%
where the time goes in v3:
time: 99.8 us; the launch traced here: 99.5 us
  blocking collectives  72.7 us (73%)
  starting transfers between devices  11.1 us (11%)
  waiting for transfers between devices  9.08 us (9%)
  local copies, waits for them, and re-layouts  2.04 us (2%)
  Pallas kernels  1.78 us (2%)
  matrix products  1.77 us (2%)
    all_to_all x4, blocking collectives, exchange(): return lax.all_to_all(array, axes, split_axis=0, concat_axis=0, tiled=True)  72.7 us
    all_to_all x1, starting transfers between devices, exchange(): return lax.all_to_all(array, axes, split_axis=0, concat_axis=0, tiled=True)  11.1 us
    all_to_all x1, waiting for transfers between devices, exchange(): return lax.all_to_all(array, axes, split_axis=0, concat_axis=0, tiled=True)  9.08 us
  transfers between devices with their start and end apart: 1, of which 1 were waited for; matrix products, arithmetic and copies ran while one was open for 0% of the time, Pallas kernels for 0%

profile of v3, /device:TPU:1, one launch (start us, length us, event | category | flops | bytes accessed | tf_op | source)
XLA Modules:
  0.0 99.5 jit_solution(3747407262001140504)
XLA Ops:
  0.6 0.0 copy-start
  0.6 0.0 copy-start.7
  0.7 1.2 %convolution_convert_fusion.2 = bf16[64,128]{1,0:T(8,128)(2,1)S(1)} fusion(bf16[64,512]{1,0:T(8,128)(2,1)} %param.9, bf16[512,128]{1,0:T(8,128)(2,1)} %param.11), kind=kOutput, calls=%fused_computation.2 | convolution fusion | flops 8396800 | bytes 212992 | tf_op jit(solution)/shard_map/dot_general | solution.py:193
  1.8 0.1 copy-done
  2.0 0.0 copy-done.7
  2.0 0.3 convolution_convert_fusion
  2.3 0.0 copy-start.1
  2.3 0.0 copy-start.2
  2.3 0.7 reshape.43
  3.0 11.1 %all-to-all-start = ((bf16[16,4,1152]{2,1,0:T(4,128)(2,1)}), bf16[16,4,1152]{2,1,0:T(4,128)(2,1)S(1)}, u32[]{:S(2)}, u32[]{:S(2)}) async-start(bf16[16,4,1152]{2,1,0:T(4,128)(2,1)} %reshape.43), calls=%async_computation | async-start | bytes 294912 | tf_op jit(solution)/shard_map/all_to_all | solution.py:28
  14.1 0.0 copy-start.3
  14.1 0.0 copy-start.4
  14.1 0.0 copy-start.5
  14.1 0.0 copy-done.1
  14.1 0.0 copy-done.2
  14.1 0.6 copy-done.3
  14.7 0.0 copy-done.4
  14.8 0.0 copy-done.5
  14.8 0.5 prepare.1
  15.2 9.1 %all-to-all-done = bf16[16,4,1152]{2,1,0:T(4,128)(2,1)S(1)} async-done(((bf16[16,4,1152]{2,1,0:T(4,128)(2,1)}), bf16[16,4,1152]{2,1,0:T(4,128)(2,1)S(1)}, u32[]{:S(2)}, u32[]{:S(2)}) %all-to-all-start) | async-done | bytes 147488 | tf_op jit(solution)/shard_map/all_to_all | solution.py:28
  24.4 0.1 reshape.44
  24.6 0.1 place.1
  24.7 29.9 %all_to_all.25.packed_ref = bf16[32,41,2,128]{3,2,1,0:T(2,128)(2,1)S(1)} all-to-all(bf16[32,41,2,128]{3,2,1,0:T(2,128)(2,1)S(1)} %place.1), channel_id=1, replica_groups=mesh['yl'=4,'z'=8,'yh'=2,'x'=4,'core'=2] {'yl','z'}, dimensions={0} | all-to-all | bytes 1343488 | tf_op jit(solution)/shard_map/all_to_all | solution.py:28
  54.6 0.0 copy-start.6
  54.6 0.6 attend.1
  55.1 14.6 %all_to_all.26 = bf16[16,10,128]{2,1,0:T(8,128)(2,1)S(1)} all-to-all(bf16[16,10,128]{2,1,0:T(8,128)(2,1)S(1)} %bitcast.27), channel_id=1, replica_groups=mesh['yl'=4,'z'=8,'yh'=2,'x'=4,'core'=2] {'z','core'}, dimensions={0} | all-to-all | bytes 81920 | tf_op jit(solution)/shard_map/all_to_all | solution.py:28
  69.8 0.1 broadcast_in_dim.14
  69.9 14.0 %all_to_all.27 = bf16[32,2,2,640]{3,1,2,0:T(2,128)(2,1)S(1)} all-to-all(bf16[32,2,2,640]{3,1,2,0:T(2,128)(2,1)S(1)} %bitcast.30), channel_id=1, replica_groups=mesh['yl'=4,'z'=8,'yh'=2,'x'=4,'core'=2] {'yh','x','yl'}, dimensions={0} | all-to-all | bytes 327680 | tf_op jit(solution)/shard_map/all_to_all | solution.py:28
  84.0 0.1 fusion.4
  84.2 0.0 copy-done.6
  84.2 0.3 convolution_convert_fusion.1
  84.6 14.3 %all_to_all.28.parts_ref = bf16[16,4,640]{2,1,0:T(4,128)(2,1)S(1)} all-to-all(bf16[16,4,640]{2,1,0:T(4,128)(2,1)S(1)} %bitcast.32), channel_id=1, replica_groups=mesh['yl'=4,'z'=8,'yh'=2,'x'=4,'core'=2] {'yh','x','core'}, dimensions={0} | all-to-all | bytes 163840 | tf_op jit(solution)/shard_map/all_to_all | solution.py:28
  98.9 0.6 finish.1
  (19 shorter events, 0.4 us)
Async XLA Ops:
  0.6 1.3 %copy-start = (bf16[512,1024]{1,0:T(8,128)(2,1)S(1)}, bf16[512,1024]{1,0:T(8,128)(2,1)}, u32[]{:S(2)}) copy-start(bf16[512,1024]{1,0:T(8,128)(2,1)} %param.10) | copy-start | bytes 3145732
  0.6 1.3 %copy-start.7 = (bf16[64,512]{1,0:T(8,128)(2,1)S(1)}, bf16[64,512]{1,0:T(8,128)(2,1)}, u32[]{:S(2)}) copy-start(bf16[64,512]{1,0:T(8,128)(2,1)} %param.9) | copy-start | bytes 196612
  2.3 11.8 %copy-start.1 = (bf16[4,32,1024]{2,1,0:T(8,128)(2,1)S(1)}, bf16[4,32,1024]{2,1,0:T(8,128)(2,1)}, u32[]{:S(2)}) copy-start(bf16[4,32,1024]{2,1,0:T(8,128)(2,1)} %keys_ref.1) | copy-start | bytes 786436
  2.3 11.8 %copy-start.2 = (bf16[4,32,1024]{2,1,0:T(8,128)(2,1)S(1)}, bf16[4,32,1024]{2,1,0:T(8,128)(2,1)}, u32[]{:S(2)}) copy-start(bf16[4,32,1024]{2,1,0:T(8,128)(2,1)} %values_ref.1) | copy-start | bytes 786436
  3.0 21.3 %all-to-all-start = ((bf16[16,4,1152]{2,1,0:T(4,128)(2,1)}), bf16[16,4,1152]{2,1,0:T(4,128)(2,1)S(1)}, u32[]{:S(2)}, u32[]{:S(2)}) async-start(bf16[16,4,1152]{2,1,0:T(4,128)(2,1)} %reshape.43), calls=%async_computation | async-start | bytes 294912 | tf_op jit(solution)/shard_map/all_to_all | solution.py:28
  14.1 0.7 copy-start.3
  14.1 0.7 copy-start.4
  14.1 0.7 copy-start.5
  54.6 29.6 %copy-start.6 = (bf16[1024,512]{1,0:T(8,128)(2,1)S(1)}, bf16[1024,512]{1,0:T(8,128)(2,1)}, u32[]{:S(2)}) copy-start(bf16[1024,512]{1,0:T(8,128)(2,1)} %param.12) | copy-start | bytes 3145732

commit v4 on v3

--- a/solution.py
+++ b/solution.py
@@ -18,9 +18,9 @@
 LOWEST = -1e30
 LIMIT = 8 * 2**20
 
-AXES = ("yl", "z", "yh", "x", "core")
-SIZES = (4, 8, 2, 4, 2)
-WIDE = ("yl", "z")
+AXES = ("far", "near", "z", "yh", "x", "core")
+SIZES = (2, 2, 8, 2, 4, 2)
+WIDE = ("far", "near", "z")
 TP = ("yh", "x", "core")
 
 
@@ -62,7 +62,7 @@
             packed_ref[place, :pairs] = keys_ref[seq, :, columns].reshape(pairs, 2, DH)
             packed_ref[place, pairs : 2 * pairs] = values_ref[seq, :, columns].reshape(pairs, 2, DH)
     lane = lax.broadcasted_iota(jnp.int32, lengths_ref.shape, 1)
-    chosen = lane == lax.axis_index("yl")
+    chosen = lane == lax.axis_index(("far", "near"))
     length = jnp.sum(jnp.where(chosen, lengths_ref[...], 0), axis=1, keepdims=True)
     position = jnp.sum(jnp.where(chosen, positions_ref[...], 0), axis=1, keepdims=True)
     valid = lax.broadcasted_iota(jnp.int32, valid_ref.shape, 1) < length
@@ -91,8 +91,13 @@
 def place_kernel(packed_ref, fresh_ref, out_ref):
     del packed_ref
     count, rows = fresh_ref.shape[:2]
-    fresh = fresh_ref[...].reshape(count, rows // 2, 2, DH)
-    out_ref[:, out_ref.shape[1] - rows // 2 :] = fresh
+    pairs = rows // 2
+    first = out_ref.shape[1] - rows
+    fresh = fresh_ref[...]
+    high = fresh.astype(out_ref.dtype)
+    low = (fresh - high.astype(jnp.float32)).astype(out_ref.dtype)
+    out_ref[:, first : first + pairs] = high.reshape(count, pairs, 2, DH)
+    out_ref[:, first + pairs :] = low.reshape(count, pairs, 2, DH)
 
 
 def place(packed, fresh):
@@ -109,16 +114,35 @@
     f32, bf16 = jnp.float32, jnp.bfloat16
     sources = packed_ref.shape[0]
     pairs = span // 2
-    sums = packed_ref[0, 2 * pairs :].reshape(-1, DH).astype(f32)
-    for source in range(1, sources):
-        sums = sums + packed_ref[source, 2 * pairs :].reshape(-1, DH).astype(f32)
-    sums = sums.astype(bf16)
-    plain = sums.astype(f32)
+    split = (2 * pairs + packed_ref.shape[1]) // 2
+    quarter = HALF // 2
+    sums = []
+    for near in range(2):
+        total = 0.0
+        for source in range(sources):
+            if source // KVH % 2 == near:
+                high = packed_ref[source, 2 * pairs : split].reshape(-1, DH).astype(f32)
+                low = packed_ref[source, split:].reshape(-1, DH).astype(f32)
+                total = total + (high + low)
+        sums.append(total.astype(bf16).astype(f32))
+    plain = jnp.concatenate(
+        [
+            sums[0][:quarter],
+            sums[1][:quarter],
+            sums[0][quarter:HALF],
+            sums[1][quarter:HALF],
+            sums[0][HALF:],
+            sums[0][HALF:],
+            sums[0][HALF:],
+            sums[0][HALF:],
+        ],
+        0,
+    )
     swapped = pltpu.roll(plain, DH // 2, 1)
     turned = (plain * turn_ref[0:1] + swapped * turn_ref[1:2]).astype(bf16)
     query = turned[:GROUP]
     new_key = turned[GROUP : GROUP + 1]
-    new_value = sums[GROUP + 1 : GROUP + 2]
+    new_value = plain[GROUP + 1 : GROUP + 2].astype(bf16)
 
     factor = DH ** (-0.5)
     keys = packed_ref[:, :pairs].reshape(-1, DH)
@@ -139,13 +163,14 @@
     for half, extra in enumerate((new_key, new_value)):
         first = half * HALF
         rows = jnp.concatenate([attention[first : first + HALF], extra, extra], 0)
+        rows = rows.reshape(HALF // 2 + 1, 2, DH)
         out_ref[:, half] = jnp.broadcast_to(rows[None], (out_ref.shape[0],) + rows.shape)
 
 
 def attend(packed, turn, valid, span):
     return call(
         functools.partial(attention_kernel, span=span),
-        jax.ShapeDtypeStruct((KVH, 2, HALF + 2, DH), jnp.bfloat16),
+        jax.ShapeDtypeStruct((KVH, 2, HALF // 2 + 1, 2, DH), jnp.bfloat16),
         [IN_VMEM] * 3,
         "attend",
     )(packed, turn, valid)
@@ -183,35 +208,40 @@
     seqs, span = cache_keys.shape[:2]
     tp = lax.axis_size(TP)
     batch = hidden_in.shape[0]
-    rows = 2 * span + GROUP + 2
+    rows = 2 * span + 2 * (HALF + 2)
     places = span * lax.axis_size(WIDE)
 
     packed, turn, valid = prepare(
         cache_keys, cache_values, frequencies(), lengths, positions, rows, places
     )
-    q_part = jnp.dot(hidden_in, q_weight, preferred_element_type=f32).astype(bf16)
-    kv_part = jnp.dot(hidden_in, kv_weight, preferred_element_type=f32).astype(bf16)
-    partial = jnp.concatenate([q_part, kv_part], 1).reshape(tp, seqs, -1)
-    partial = exchange(partial, TP)
-
-    q_rows = partial[:, :, : HALF * DH].reshape(KVH, 2, seqs, HALF, DH)
-    q_rows = q_rows.transpose(2, 0, 1, 3, 4).reshape(seqs, KVH, GROUP, DH)
-    kv_rows = partial[:, :, HALF * DH :].reshape(2, KVH, seqs, DH).transpose(2, 1, 0, 3)
+    q_part = jnp.dot(hidden_in, q_weight, preferred_element_type=f32)
+    kv_part = jnp.dot(hidden_in, kv_weight, preferred_element_type=f32)
+    middle = HALF * DH // 2
+    partial = jnp.stack(
+        [
+            jnp.concatenate([q_part[:, :middle], kv_part], 1),
+            jnp.concatenate([q_part[:, middle:], jnp.zeros_like(kv_part)], 1),
+        ]
+    )
+    partial = exchange(partial.reshape(2 * tp, seqs, -1), ("near",) + TP)
+    partial = jnp.sum(partial.reshape(2, tp, seqs, -1), 0)
+
+    q_rows = partial[:, :, :middle].reshape(KVH, 2, seqs, HALF // 2, DH)
+    q_rows = q_rows.transpose(2, 0, 1, 3, 4).reshape(seqs, KVH, HALF, DH)
+    kv_rows = partial[:, :, middle:].reshape(2, KVH, seqs, DH).transpose(2, 1, 0, 3)
     fresh = jnp.concatenate([q_rows, kv_rows], 2)
     packed = place(packed, fresh.reshape(seqs * KVH, -1, DH))
     packed = exchange(packed, WIDE)
     heads = attend(packed, turn, valid, span)
 
     heads = exchange(heads.reshape((KVH * 2,) + heads.shape[2:]), ("z", "core"))
-    middle = HALF * DH // 2
-    mixed = heads[:, :HALF].reshape(KVH, 2, 2, middle)
-    fresh = heads[:, HALF : HALF + 2].reshape(KVH, 2, 2, DH)
-    piece = jnp.concatenate([mixed, fresh], 3)
-    piece = jnp.broadcast_to(piece[:, None], (KVH, seqs) + piece.shape[1:])
-    piece = exchange(piece.reshape((KVH * seqs,) + piece.shape[2:]), ("yh", "x", "yl"))
-    flat = jnp.concatenate([piece[:, :, 0, :middle], piece[:, :, 1, :middle]], 2)
-    product = jnp.dot(flat.reshape(batch, -1), o_weight, preferred_element_type=f32).astype(bf16)
-    out = jnp.concatenate([product, piece[:, :, 0, middle:].reshape(batch, -1)], 1)
+    piece = heads.reshape((KVH, 1, -1) + heads.shape[2:])
+    piece = jnp.broadcast_to(piece, (KVH, seqs) + piece.shape[2:])
+    piece = exchange(piece.reshape((KVH * seqs,) + piece.shape[2:]), ("yh", "x", "far", "near"))
+    piece = piece.reshape(batch, HALF + 2, DH)
+    flat = piece[:, :HALF].reshape(batch, -1)
+    product = jnp.dot(flat, o_weight, preferred_element_type=f32).astype(bf16)
+    out = jnp.concatenate([product, piece[:, HALF]], 1)
     out = out.reshape(KVH, seqs, 2, -1).transpose(0, 2, 1, 3).reshape(tp, seqs, -1)
     out = exchange(out, TP)
     return finish(out, o_weight.shape[1])

time: 99.8 us -> 104 us (1.042)
  waiting for transfers between devices: 9.08 us -> 13.1 us
    all_to_all x1, waiting for transfers between devices: 9.08 us -> 13.1 us  [exchange(): return lax.all_to_all(array, axes, split_axis=0, concat_axis=0, tiled=True)]
where the time goes in v4:
time: 104 us; the launch traced here: 103 us
  blocking collectives  72.2 us (69%)
  waiting for transfers between devices  13.1 us (13%)
  starting transfers between devices  11.3 us (11%)
  local copies, waits for them, and re-layouts  2.02 us (2%)
  Pallas kernels  1.78 us (2%)
  matrix products  1.77 us (2%)
    all_to_all x4, blocking collectives, exchange(): return lax.all_to_all(array, axes, split_axis=0, concat_axis=0, tiled=True)  72.2 us
    all_to_all x1, waiting for transfers between devices, exchange(): return lax.all_to_all(array, axes, split_axis=0, concat_axis=0, tiled=True)  13.1 us
    all_to_all x1, starting transfers between devices, exchange(): return lax.all_to_all(array, axes, split_axis=0, concat_axis=0, tiled=True)  11.3 us
  transfers between devices with their start and end apart: 1, of which 1 were waited for; matrix products, arithmetic and copies ran while one was open for 0% of the time, Pallas kernels for 0%

profile of v4, /device:TPU:1, one launch (start us, length us, event | category | flops | bytes accessed | tf_op | source)
XLA Modules:
  0.0 103.3 jit_solution(17407861188760291444)
XLA Ops:
  0.6 0.0 copy-start
  0.6 0.0 copy-start.7
  0.7 1.2 %fusion.4 = f32[64,128]{1,0:T(8,128)S(1)} fusion(bf16[64,512]{1,0:T(8,128)(2,1)} %param.9, bf16[512,128]{1,0:T(8,128)(2,1)} %param.11), kind=kOutput, calls=%fused_computation.11 | convolution fusion | flops 8388608 | bytes 229376 | tf_op jit(solution)/shard_map/dot_general | solution.py:218
  1.8 0.1 copy-done
  2.0 0.0 copy-done.7
  2.0 0.3 fusion.3
  2.4 0.8 reshape.42
  3.2 0.0 copy-start.1
  3.2 0.0 copy-start.2
  3.2 11.3 %all-to-all-start = ((f32[32,4,640]{2,1,0:T(4,128)}), f32[32,4,640]{2,1,0:T(4,128)S(1)}, u32[]{:S(2)}, u32[]{:S(2)}) async-start(f32[32,4,640]{2,1,0:T(4,128)} %reshape.42), calls=%async_computation | async-start | bytes 655360 | tf_op jit(solution)/shard_map/all_to_all | solution.py:28
  14.5 0.0 copy-start.3
  14.6 0.0 copy-start.4
  14.6 0.0 copy-start.5
  14.6 0.0 copy-done.1
  14.6 0.0 copy-done.2
  14.6 0.6 copy-done.3
  15.2 0.0 copy-done.4
  15.2 0.0 copy-done.5
  15.2 0.5 prepare.1
  15.7 13.1 %all-to-all-done = f32[32,4,640]{2,1,0:T(4,128)S(1)} async-done(((f32[32,4,640]{2,1,0:T(4,128)}), f32[32,4,640]{2,1,0:T(4,128)S(1)}, u32[]{:S(2)}, u32[]{:S(2)}) %all-to-all-start) | async-done | bytes 327712 | tf_op jit(solution)/shard_map/all_to_all | solution.py:28
  28.8 0.1 reduce_sum.9
  28.9 0.1 reshape.44
  29.1 0.1 place.1
  29.2 30.5 %all_to_all.25.packed_ref = bf16[32,42,2,128]{3,2,1,0:T(2,128)(2,1)S(1)} all-to-all(bf16[32,42,2,128]{3,2,1,0:T(2,128)(2,1)S(1)} %place.1), channel_id=1, replica_groups=mesh['far'=2,'near'=2,'z'=8,'yh'=2,'x'=4,'core'=2] {'far','near','z'}, dimensions={0} | all-to-all | bytes 1376256 | tf_op jit(solution)/shard_map/all_to_all | solution.py:28
  59.7 0.0 copy-start.6
  59.7 0.6 attend.1
  60.3 13.7 %all_to_all.26 = bf16[16,5,2,128]{3,2,1,0:T(2,128)(2,1)S(1)} all-to-all(bf16[16,5,2,128]{3,2,1,0:T(2,128)(2,1)S(1)} %bitcast.32), channel_id=1, replica_groups=mesh['far'=2,'near'=2,'z'=8,'yh'=2,'x'=4,'core'=2] {'z','core'}, dimensions={0} | all-to-all | bytes 81920 | tf_op jit(solution)/shard_map/all_to_all | solution.py:28
  74.0 0.1 broadcast_in_dim.17
  74.1 13.6 %all_to_all.27 = bf16[32,10,2,128]{3,2,1,0:T(2,128)(2,1)S(1)} all-to-all(bf16[32,10,2,128]{3,2,1,0:T(2,128)(2,1)S(1)} %bitcast.36), channel_id=1, replica_groups=mesh['far'=2,'near'=2,'z'=8,'yh'=2,'x'=4,'core'=2] {'yh','x','far','near'}, dimensions={0} | all-to-all | bytes 327680 | tf_op jit(solution)/shard_map/all_to_all | solution.py:28
  87.7 0.1 reshape.48
  87.8 0.0 copy-done.6
  87.8 0.3 convolution_convert_fusion
  88.3 14.4 %all_to_all.28.parts_ref = bf16[16,4,640]{2,1,0:T(4,128)(2,1)S(1)} all-to-all(bf16[16,4,640]{2,1,0:T(4,128)(2,1)S(1)} %bitcast.39), channel_id=1, replica_groups=mesh['far'=2,'near'=2,'z'=8,'yh'=2,'x'=4,'core'=2] {'yh','x','core'}, dimensions={0} | all-to-all | bytes 163840 | tf_op jit(solution)/shard_map/all_to_all | solution.py:28
  102.7 0.6 finish.1
  (16 shorter events, 0.3 us)
Async XLA Ops:
  0.6 1.3 %copy-start = (bf16[512,1024]{1,0:T(8,128)(2,1)S(1)}, bf16[512,1024]{1,0:T(8,128)(2,1)}, u32[]{:S(2)}) copy-start(bf16[512,1024]{1,0:T(8,128)(2,1)} %param.10) | copy-start | bytes 3145732
  0.6 1.3 %copy-start.7 = (bf16[64,512]{1,0:T(8,128)(2,1)S(1)}, bf16[64,512]{1,0:T(8,128)(2,1)}, u32[]{:S(2)}) copy-start(bf16[64,512]{1,0:T(8,128)(2,1)} %param.9) | copy-start | bytes 196612
  3.2 11.4 %copy-start.1 = (bf16[4,32,1024]{2,1,0:T(8,128)(2,1)S(1)}, bf16[4,32,1024]{2,1,0:T(8,128)(2,1)}, u32[]{:S(2)}) copy-start(bf16[4,32,1024]{2,1,0:T(8,128)(2,1)} %keys_ref.1) | copy-start | bytes 786436
  3.2 11.4 %copy-start.2 = (bf16[4,32,1024]{2,1,0:T(8,128)(2,1)S(1)}, bf16[4,32,1024]{2,1,0:T(8,128)(2,1)}, u32[]{:S(2)}) copy-start(bf16[4,32,1024]{2,1,0:T(8,128)(2,1)} %values_ref.1) | copy-start | bytes 786436
  3.2 25.6 %all-to-all-start = ((f32[32,4,640]{2,1,0:T(4,128)}), f32[32,4,640]{2,1,0:T(4,128)S(1)}, u32[]{:S(2)}, u32[]{:S(2)}) async-start(f32[32,4,640]{2,1,0:T(4,128)} %reshape.42), calls=%async_computation | async-start | bytes 655360 | tf_op jit(solution)/shard_map/all_to_all | solution.py:28
  14.5 0.7 copy-start.3
  14.6 0.7 copy-start.4
  14.6 0.7 copy-start.5
  59.7 28.1 %copy-start.6 = (bf16[1024,512]{1,0:T(8,128)(2,1)S(1)}, bf16[1024,512]{1,0:T(8,128)(2,1)}, u32[]{:S(2)}) copy-start(bf16[1024,512]{1,0:T(8,128)(2,1)} %param.12) | copy-start | bytes 3145732
